TPU v7x, 32 devices: a whole 2x2x4 slice. The times are simulated.
32 devices in a mesh: groups: 2 (over x), dp: 16 (over z, y, core).
Axes of the slice: x: 2, y: 2, z: 4, core: 2. Of those that a mesh axis runs over, the one named last changes fastest.
Arguments:
- points: bfloat16 [131072, 128], P(('groups', 'dp')), parts along dimension 0, may hold values from -0.52 to 0.52
- probes: bfloat16 [16, 131072], P(None, ('groups', 'dp')), parts along dimension 1, may hold values from -6 to 6
- round_masks: int32 [6], P('groups'), parts along dimension 0, may hold values from 1 to 15, as said below
Outputs:
- product: float32 [16, 131072], P(None, ('groups', 'dp')), parts along dimension 1
There are 2 independent parts, one for each index of `groups`. A program takes and returns all parts, laid end to end along the dimension named above; each array names one. Nothing has to cross between parts.
Inputs may be any that keep to these rules, and one draw needn't show every extreme that they name: `round_masks`: the 3 masks are distinct; one of them equals 15.
All inputs are finite; a program needn't handle non-finite values.
Results may differ from a plain program's by a relative error of at most 0.0028.
Values may be sent and summed in bfloat16 or wider, within the bound.
A program may use at most 64 MiB of HBM per device.

v0:
```python
import jax
import jax.numpy as jnp
from jax import lax
from jax.sharding import PartitionSpec as P

GAMMA = 2.0
NOISE = 0.25


def partner(value, axis, bit):
    mask = 2**bit
    pairs = [(source, source ^ mask) for source in range(lax.axis_size(axis))]
    return lax.ppermute(value, axis, pairs)


def point_norms(rows):
    return jnp.sum(jnp.square(rows.astype(jnp.float32)), axis=1)


def kernel_block(row_x, row_n, col_x, col_n):
    dots = lax.dot_general(
        row_x, col_x, (((1,), (1,)), ((), ())), preferred_element_type=jnp.float32
    )
    return jnp.exp(-GAMMA * (row_n[:, None] + col_n[None, :] - 2.0 * dots)).astype(jnp.bfloat16)


def tile_product(row_x, row_n, row_v, col_x, col_n, col_v, need_cols):
    rows = row_x.shape[0]
    cols = col_x.shape[0]
    width = row_x.shape[1]
    probe_count = row_v.shape[0]
    row_blk = min(1024, rows)
    n_rb = rows // row_blk
    rx_blocks = row_x.reshape(n_rb, row_blk, width)
    rn_blocks = row_n.reshape(n_rb, row_blk)
    rv_blocks = row_v.reshape(probe_count, n_rb, row_blk).transpose(1, 0, 2)

    def row_step(col_total, row_piece):
        block_x, block_n, block_v = row_piece
        kern = kernel_block(block_x, block_n, col_x, col_n)
        row_sum = lax.dot_general(
            col_v, kern, (((1,), (1,)), ((), ())), preferred_element_type=jnp.float32
        )
        if need_cols:
            col_total = col_total + jnp.dot(block_v, kern, preferred_element_type=jnp.float32)
        return (col_total, row_sum)

    start_cols = jnp.zeros((probe_count, cols if need_cols else 0), jnp.float32)
    col_total, row_sums = lax.scan(row_step, start_cols, (rx_blocks, rn_blocks, rv_blocks))
    row_result = row_sums.transpose(1, 0, 2).reshape(probe_count, rows)
    if need_cols:
        col_result = col_total
    else:
        col_result = None
    return (row_result, col_result)


def fetch_partner(pair, mask, bit_list):
    for bit in bit_list:
        bitset = mask >> bit & 1 == 1
        moved = partner((pair[0], pair[1]), "dp", bit)
        pair = (jnp.where(bitset, moved[0], pair[0]), jnp.where(bitset, moved[1], pair[1]))
    return pair


def return_partials(term, mask, bit_list):
    for bit in bit_list:
        bitset = mask >> bit & 1 == 1
        moved = partner(term, "dp", bit)
        term = jnp.where(bitset, moved, term)
    return term


def on_device(points, probes, round_masks):
    own_n = point_norms(points)
    index_here = lax.axis_index("dp")
    nbits = lax.axis_size("dp").bit_length() - 1
    bit_list = list(range(nbits))
    size_here = points.shape[0]
    probe_count = probes.shape[0]
    diag_rows, unused = tile_product(points, own_n, probes, points, own_n, probes, False)
    total = NOISE * probes.astype(jnp.float32) + diag_rows
    for step in range(round_masks.shape[0]):
        mask = round_masks[step]
        far_x, far_v = fetch_partner((points, probes), mask, bit_list)
        far_n = point_norms(far_x)
        lower = index_here < jnp.bitwise_xor(index_here, mask)

        def compute_tile():
            return tile_product(points, own_n, probes, far_x, far_n, far_v, True)

        def skip_tile():
            empty = jnp.zeros((probe_count, size_here), jnp.float32)
            return (empty, empty)

        row_part, col_part = lax.cond(lower, compute_tile, skip_tile)
        total = total + row_part + return_partials(col_part, mask, bit_list)
    return total


def solution(mesh):
    in_specs = (P(("groups", "dp"), None), P(None, ("groups", "dp")), P("groups"))
    out_specs = P(None, ("groups", "dp"))
    return jax.shard_map(
        on_device, mesh=mesh, in_specs=in_specs, out_specs=out_specs, check_vma=False
    )
```

profile of v0, /device:TPU:0, one launch (start us, length us, event | category | flops | bytes accessed | tf_op | source)
XLA Modules:
  0.0 499.1 jit_solution(13246512360619434236)
XLA Ops:
  38.3 19.8 %collective-permute-done.1 = bf16[4096,128]{1,0:T(8,128)(2,1)S(1)} collective-permute-done((bf16[4096,128]{1,0:T(8,128)(2,1)S(1)}, bf16[4096,128]{1,0:T(8,128)(2,1)S(1)}, u32[]{:S(2)}, u32[]{:S(2)}) %collective-permute-start.1) | collective-permute-done | bytes 1048608 | tf_op jit(solution)/shard_map/ppermute | solution.py:13
  58.9 21.7 %collective-permute-done.12 = bf16[4096,128]{1,0:T(8,128)(2,1)S(1)} collective-permute-done((bf16[4096,128]{1,0:T(8,128)(2,1)S(1)}, bf16[4096,128]{1,0:T(8,128)(2,1)S(1)}, u32[]{:S(2)}, u32[]{:S(2)}) %collective-permute-start.12) | collective-permute-done | bytes 1048608 | tf_op jit(solution)/shard_map/ppermute | solution.py:13
  81.3 19.0 %collective-permute-done.22 = bf16[4096,128]{1,0:T(8,128)(2,1)S(1)} collective-permute-done((bf16[4096,128]{1,0:T(8,128)(2,1)S(1)}, bf16[4096,128]{1,0:T(8,128)(2,1)S(1)}, u32[]{:S(2)}, u32[]{:S(2)}) %collective-permute-start.22) | collective-permute-done | bytes 1048608 | tf_op jit(solution)/shard_map/ppermute | solution.py:13
  102.6 35.0 %collective-permute-done.13 = bf16[4096,128]{1,0:T(8,128)(2,1)S(1)} collective-permute-done((bf16[4096,128]{1,0:T(8,128)(2,1)S(1)}, bf16[4096,128]{1,0:T(8,128)(2,1)S(1)}, u32[]{:S(2)}, u32[]{:S(2)}) %collective-permute-start.13) | collective-permute-done | bytes 1048608 | tf_op jit(solution)/shard_map/ppermute | solution.py:13
  138.8 21.0 %collective-permute-done.23 = bf16[4096,128]{1,0:T(8,128)(2,1)S(1)} collective-permute-done((bf16[4096,128]{1,0:T(8,128)(2,1)S(1)}, bf16[4096,128]{1,0:T(8,128)(2,1)S(1)}, u32[]{:S(2)}, u32[]{:S(2)}) %collective-permute-start.23) | collective-permute-done | bytes 1048608 | tf_op jit(solution)/shard_map/ppermute | solution.py:13
  160.9 56.0 %collective-permute-done.3 = bf16[4096,128]{1,0:T(8,128)(2,1)S(1)} collective-permute-done((bf16[4096,128]{1,0:T(8,128)(2,1)S(1)}, bf16[4096,128]{1,0:T(8,128)(2,1)S(1)}, u32[]{:S(2)}, u32[]{:S(2)}) %collective-permute-start.3) | collective-permute-done | bytes 1048608 | tf_op jit(solution)/shard_map/ppermute | solution.py:13
  218.7 70.5 %conditional.3 = (f32[16,4096]{1,0:T(8,128)S(1)}, f32[16,4096]{1,0:T(8,128)}) conditional(s32[]{:T(128)} %convert_element_type.38, () %tuple.46, (bf16[4096,128]{1,0:T(8,128)(2,1)S(1)}, f32[4096]{0:T(1024)S(1)}, bf16[16,4096]{1,0:T(8,128)(2,1)S(1)}, f32[4096,128]{1,0:T(8,128)S(1)}, bf16[4096,128]{1,0:T(8,128)(2,1)}, ...), branch_computations={%region_4.5_spmd, %region_5.8_spmd} | conditional | flops 1364389888 | bytes 57127772 | solution.py:96
  222.7 65.5 %while.46 = (s32[]{:T(128)}, f32[16,4096]{1,0:T(8,128)}, f32[4,16,1024]{2,1,0:T(8,128)}, bf16[4,16,1024]{2,1,0:T(8,128)(2,1)S(1)}, f32[4,1024]{1,0:T(4,128)S(1)}...) while((s32[]{:T(128)}, f32[16,4096]{1,0:T(8,128)}, ...), condition=%wide.region_7.7_spmd.clone, body=%wide.region_6.6_spmd.clone.sunk | while | flops 1363279872 | bytes 52425392 | solution.py:49
  222.7 7.5 %exponential_convert_fusion.9 = bf16[1024,4096]{1,0:T(8,128)(2,1)} fusion(bf16[4096,128]{1,0:T(8,128)(2,1)} %get-tuple-element.774, f32[4096]{0:T(1024)} %get-tuple-element.772, f32[1024]{0:T(1024)S(1)} %bitcast.168, bf16[4,1024,128]{2,1,0:T(8,128)(2,1)S(1)} %get-tuple-element.773, s32[]{:T(128)} %get-tuple-element.756), kind=kOutput, calls=%fused_computation.10.clone.1 | convolution fusion | flops 1094713344 | bytes 9719812 | tf_op jit(solution)/shard_map/cond/branch_1_fun/while/body/eval_jaxpr/dot_general | solution.py:21
  239.1 7.5 %exponential_convert_fusion.9 = bf16[1024,4096]{1,0:T(8,128)(2,1)} fusion(bf16[4096,128]{1,0:T(8,128)(2,1)} %get-tuple-element.774, f32[4096]{0:T(1024)} %get-tuple-element.772, f32[1024]{0:T(1024)S(1)} %bitcast.168, bf16[4,1024,128]{2,1,0:T(8,128)(2,1)S(1)} %get-tuple-element.773, s32[]{:T(128)} %get-tuple-element.756), kind=kOutput, calls=%fused_computation.10.clone.1 | convolution fusion | flops 1094713344 | bytes 9719812 | tf_op jit(solution)/shard_map/cond/branch_1_fun/while/body/eval_jaxpr/dot_general | solution.py:21
  255.4 7.4 %exponential_convert_fusion.9 = bf16[1024,4096]{1,0:T(8,128)(2,1)} fusion(bf16[4096,128]{1,0:T(8,128)(2,1)} %get-tuple-element.774, f32[4096]{0:T(1024)} %get-tuple-element.772, f32[1024]{0:T(1024)S(1)} %bitcast.168, bf16[4,1024,128]{2,1,0:T(8,128)(2,1)S(1)} %get-tuple-element.773, s32[]{:T(128)} %get-tuple-element.756), kind=kOutput, calls=%fused_computation.10.clone.1 | convolution fusion | flops 1094713344 | bytes 9719812 | tf_op jit(solution)/shard_map/cond/branch_1_fun/while/body/eval_jaxpr/dot_general | solution.py:21
  271.8 7.4 %exponential_convert_fusion.9 = bf16[1024,4096]{1,0:T(8,128)(2,1)} fusion(bf16[4096,128]{1,0:T(8,128)(2,1)} %get-tuple-element.774, f32[4096]{0:T(1024)} %get-tuple-element.772, f32[1024]{0:T(1024)S(1)} %bitcast.168, bf16[4,1024,128]{2,1,0:T(8,128)(2,1)S(1)} %get-tuple-element.773, s32[]{:T(128)} %get-tuple-element.756), kind=kOutput, calls=%fused_computation.10.clone.1 | convolution fusion | flops 1094713344 | bytes 9719812 | tf_op jit(solution)/shard_map/cond/branch_1_fun/while/body/eval_jaxpr/dot_general | solution.py:21
  293.0 68.9 %conditional.4 = (f32[16,4096]{1,0:T(8,128)S(1)}, f32[16,4096]{1,0:T(8,128)}) conditional(s32[]{:T(128)} %convert_element_type.40, () %tuple.48, (bf16[4096,128]{1,0:T(8,128)(2,1)S(1)}, f32[4096]{0:T(1024)S(1)}, bf16[16,4096]{1,0:T(8,128)(2,1)S(1)}, f32[4096,128]{1,0:T(8,128)S(1)}, bf16[4096,128]{1,0:T(8,128)(2,1)}, ...), branch_computations={%region_9.10_spmd, %region_10.13_spmd} | conditional | flops 1364389888 | bytes 56079140 | solution.py:96
  295.5 65.5 %while.47 = (s32[]{:T(128)}, f32[16,4096]{1,0:T(8,128)}, f32[4,16,1024]{2,1,0:T(8,128)}, bf16[4,16,1024]{2,1,0:T(8,128)(2,1)S(1)}, f32[4,1024]{1,0:T(4,128)S(1)}...) while((s32[]{:T(128)}, f32[16,4096]{1,0:T(8,128)}, ...), condition=%wide.region_12.12_spmd.clone, body=%wide.region_11.11_spmd.clone.sunk | while | flops 1363279872 | bytes 52425392 | solution.py:49
  295.5 7.4 %exponential_convert_fusion.8 = bf16[1024,4096]{1,0:T(8,128)(2,1)} fusion(bf16[4096,128]{1,0:T(8,128)(2,1)} %get-tuple-element.741, f32[4096]{0:T(1024)} %get-tuple-element.739, f32[1024]{0:T(1024)S(1)} %bitcast.169, bf16[4,1024,128]{2,1,0:T(8,128)(2,1)S(1)} %get-tuple-element.740, s32[]{:T(128)} %get-tuple-element.723), kind=kOutput, calls=%fused_computation.22.clone.1 | convolution fusion | flops 1094713344 | bytes 9719812 | tf_op jit(solution)/shard_map/cond/branch_1_fun/while/body/eval_jaxpr/dot_general | solution.py:21
  311.8 7.5 %exponential_convert_fusion.8 = bf16[1024,4096]{1,0:T(8,128)(2,1)} fusion(bf16[4096,128]{1,0:T(8,128)(2,1)} %get-tuple-element.741, f32[4096]{0:T(1024)} %get-tuple-element.739, f32[1024]{0:T(1024)S(1)} %bitcast.169, bf16[4,1024,128]{2,1,0:T(8,128)(2,1)S(1)} %get-tuple-element.740, s32[]{:T(128)} %get-tuple-element.723), kind=kOutput, calls=%fused_computation.22.clone.1 | convolution fusion | flops 1094713344 | bytes 9719812 | tf_op jit(solution)/shard_map/cond/branch_1_fun/while/body/eval_jaxpr/dot_general | solution.py:21
  344.5 7.4 %exponential_convert_fusion.8 = bf16[1024,4096]{1,0:T(8,128)(2,1)} fusion(bf16[4096,128]{1,0:T(8,128)(2,1)} %get-tuple-element.741, f32[4096]{0:T(1024)} %get-tuple-element.739, f32[1024]{0:T(1024)S(1)} %bitcast.169, bf16[4,1024,128]{2,1,0:T(8,128)(2,1)S(1)} %get-tuple-element.740, s32[]{:T(128)} %get-tuple-element.723), kind=kOutput, calls=%fused_computation.22.clone.1 | convolution fusion | flops 1094713344 | bytes 9719812 | tf_op jit(solution)/shard_map/cond/branch_1_fun/while/body/eval_jaxpr/dot_general | solution.py:21
  365.7 69.1 %conditional.5 = (f32[16,4096]{1,0:T(8,128)S(1)}, f32[16,4096]{1,0:T(8,128)}) conditional(s32[]{:T(128)} %convert_element_type.42, () %tuple.50, (bf16[4096,128]{1,0:T(8,128)(2,1)S(1)}, f32[4096]{0:T(1024)S(1)}, bf16[16,4096]{1,0:T(8,128)(2,1)S(1)}, f32[4096,128]{1,0:T(8,128)S(1)}, bf16[4096,128]{1,0:T(8,128)(2,1)}, ...), branch_computations={%region_14.15_spmd, %region_15.18_spmd} | conditional | flops 1364389888 | bytes 56079140 | solution.py:96
  368.1 65.5 %while.48 = (s32[]{:T(128)}, f32[16,4096]{1,0:T(8,128)}, f32[4,16,1024]{2,1,0:T(8,128)}, bf16[4,16,1024]{2,1,0:T(8,128)(2,1)S(1)}, f32[4,1024]{1,0:T(4,128)S(1)}...) while((s32[]{:T(128)}, f32[16,4096]{1,0:T(8,128)}, ...), condition=%wide.region_17.17_spmd.clone, body=%wide.region_16.16_spmd.clone.sunk | while | flops 1363279872 | bytes 52425392 | solution.py:49
  368.1 7.5 %exponential_convert_fusion.7 = bf16[1024,4096]{1,0:T(8,128)(2,1)} fusion(bf16[4096,128]{1,0:T(8,128)(2,1)} %get-tuple-element.708, f32[4096]{0:T(1024)} %get-tuple-element.706, f32[1024]{0:T(1024)S(1)} %bitcast.170, bf16[4,1024,128]{2,1,0:T(8,128)(2,1)S(1)} %get-tuple-element.707, s32[]{:T(128)} %get-tuple-element.690), kind=kOutput, calls=%fused_computation.34.clone.1 | convolution fusion | flops 1094713344 | bytes 9719812 | tf_op jit(solution)/shard_map/cond/branch_1_fun/while/body/eval_jaxpr/dot_general | solution.py:21
  384.5 7.5 %exponential_convert_fusion.7 = bf16[1024,4096]{1,0:T(8,128)(2,1)} fusion(bf16[4096,128]{1,0:T(8,128)(2,1)} %get-tuple-element.708, f32[4096]{0:T(1024)} %get-tuple-element.706, f32[1024]{0:T(1024)S(1)} %bitcast.170, bf16[4,1024,128]{2,1,0:T(8,128)(2,1)S(1)} %get-tuple-element.707, s32[]{:T(128)} %get-tuple-element.690), kind=kOutput, calls=%fused_computation.34.clone.1 | convolution fusion | flops 1094713344 | bytes 9719812 | tf_op jit(solution)/shard_map/cond/branch_1_fun/while/body/eval_jaxpr/dot_general | solution.py:21
  400.8 7.5 %exponential_convert_fusion.7 = bf16[1024,4096]{1,0:T(8,128)(2,1)} fusion(bf16[4096,128]{1,0:T(8,128)(2,1)} %get-tuple-element.708, f32[4096]{0:T(1024)} %get-tuple-element.706, f32[1024]{0:T(1024)S(1)} %bitcast.170, bf16[4,1024,128]{2,1,0:T(8,128)(2,1)S(1)} %get-tuple-element.707, s32[]{:T(128)} %get-tuple-element.690), kind=kOutput, calls=%fused_computation.34.clone.1 | convolution fusion | flops 1094713344 | bytes 9719812 | tf_op jit(solution)/shard_map/cond/branch_1_fun/while/body/eval_jaxpr/dot_general | solution.py:21
  417.2 7.5 %exponential_convert_fusion.7 = bf16[1024,4096]{1,0:T(8,128)(2,1)} fusion(bf16[4096,128]{1,0:T(8,128)(2,1)} %get-tuple-element.708, f32[4096]{0:T(1024)} %get-tuple-element.706, f32[1024]{0:T(1024)S(1)} %bitcast.170, bf16[4,1024,128]{2,1,0:T(8,128)(2,1)S(1)} %get-tuple-element.707, s32[]{:T(128)} %get-tuple-element.690), kind=kOutput, calls=%fused_computation.34.clone.1 | convolution fusion | flops 1094713344 | bytes 9719812 | tf_op jit(solution)/shard_map/cond/branch_1_fun/while/body/eval_jaxpr/dot_general | solution.py:21
  465.3 31.9 %while.49 = (s32[]{:T(128)}, f32[4,16,1024]{2,1,0:T(8,128)}, f32[4,1024]{1,0:T(4,128)}, f32[4096]{0:T(1024)S(1)}, bf16[4,1024,128]{2,1,0:T(8,128)(2,1)S(1)}, /*i...) while((s32[]{:T(128)}, f32[4,16,1024]{2,1,0:T(8,128)}, f32[4,1024]{1,0:T(4,128)}, ...), condition=%wide.region_2.3_spmd, body=%wide.region_1.2_spmd.sunk | while | flops 1228931072 | bytes 1537113 | solution.py:49
  (242 shorter events, 234.1 us)
Async XLA Ops:
  0.0 11.8 %collective-permute-start.4 = (bf16[16,4096]{1,0:T(8,128)(2,1)}, bf16[16,4096]{1,0:T(8,128)(2,1)S(1)}, u32[]{:S(2)}, u32[]{:S(2)}) collective-permute-start(bf16[16,4096]{1,0:T(8,128)(2,1)} %param.18), channel_id=1, source_target_pairs={{0,1},{1,0},{2,3},{3,2},{4,5},{5,4},{6,7},{7,6},{8,9},{9,8},{10,11... | collective-permute-start | bytes 393224 | tf_op jit(solution)/shard_map/ppermute | solution.py:13
  0.5 30.1 %collective-permute-start = (bf16[4096,128]{1,0:T(8,128)(2,1)}, bf16[4096,128]{1,0:T(8,128)(2,1)S(1)}, u32[]{:S(2)}, u32[]{:S(2)}) collective-permute-start(bf16[4096,128]{1,0:T(8,128)(2,1)} %param.17), channel_id=1, source_target_pairs={{0,1},{1,0},{2,3},{3,2},{4,5},{5,4},{6,7},{7,6},{8,9},{9,8},{10,11... | collective-permute-start | bytes 3145736 | tf_op jit(solution)/shard_map/ppermute | solution.py:13
  26.3 9.3 %collective-permute-start.26 = (bf16[16,4096]{1,0:T(8,128)(2,1)S(1)}, bf16[16,4096]{1,0:T(8,128)(2,1)S(1)}, u32[]{:S(2)}, u32[]{:S(2)}) collective-permute-start(bf16[16,4096]{1,0:T(8,128)(2,1)S(1)} %broadcast_select_fusion.15), channel_id=1, source_target_pairs={{0,4},{1,5},{2,6},{3,7},{4,0},{5,1},{6,2},{7,3},{8,12},{9,13},{10,... | collective-permute-start | bytes 393224 | tf_op jit(solution)/shard_map/ppermute | solution.py:13
  27.9 190.2 %collective-permute-start.7 = (bf16[16,4096]{1,0:T(8,128)(2,1)S(1)}, bf16[16,4096]{1,0:T(8,128)(2,1)S(1)}, u32[]{:S(2)}, u32[]{:S(2)}) collective-permute-start(bf16[16,4096]{1,0:T(8,128)(2,1)S(1)} %broadcast_select_fusion.29), channel_id=1, source_target_pairs={{0,8},{1,9},{2,10},{3,11},{4,12},{5,13},{6,14},{7,15},{8,0},{9,1},... | collective-permute-start | bytes 393224 | tf_op jit(solution)/shard_map/ppermute | solution.py:13
  31.9 26.2 %collective-permute-start.1 = (bf16[4096,128]{1,0:T(8,128)(2,1)S(1)}, bf16[4096,128]{1,0:T(8,128)(2,1)S(1)}, u32[]{:S(2)}, u32[]{:S(2)}) collective-permute-start(bf16[4096,128]{1,0:T(8,128)(2,1)S(1)} %get-tuple-element.462), channel_id=1, source_target_pairs={{0,2},{1,3},{2,0},{3,1},{4,6},{5,7},{6,4},{7,5},{8,10},{9,11},{10,... | collective-permute-start | bytes 3145736 | tf_op jit(solution)/shard_map/ppermute | solution.py:13
  33.3 259.0 %collective-permute-start.17 = (bf16[16,4096]{1,0:T(8,128)(2,1)}, bf16[16,4096]{1,0:T(8,128)(2,1)}, u32[]{:S(2)}, u32[]{:S(2)}) collective-permute-start(bf16[16,4096]{1,0:T(8,128)(2,1)} %broadcast_select_fusion.23), channel_id=1, source_target_pairs={{0,8},{1,9},{2,10},{3,11},{4,12},{5,13},{6,14},{7,15},{8,0},{9,1},... | collective-permute-start | bytes 393224 | tf_op jit(solution)/shard_map/ppermute | solution.py:13
  34.6 46.0 %collective-permute-start.12 = (bf16[4096,128]{1,0:T(8,128)(2,1)S(1)}, bf16[4096,128]{1,0:T(8,128)(2,1)S(1)}, u32[]{:S(2)}, u32[]{:S(2)}) collective-permute-start(bf16[4096,128]{1,0:T(8,128)(2,1)S(1)} %get-tuple-element.464), channel_id=1, source_target_pairs={{0,2},{1,3},{2,0},{3,1},{4,6},{5,7},{6,4},{7,5},{8,10},{9,11},{10,... | collective-permute-start | bytes 3145736 | tf_op jit(solution)/shard_map/ppermute | solution.py:13
  36.3 328.7 %collective-permute-start.27 = (bf16[16,4096]{1,0:T(8,128)(2,1)}, bf16[16,4096]{1,0:T(8,128)(2,1)}, u32[]{:S(2)}, u32[]{:S(2)}) collective-permute-start(bf16[16,4096]{1,0:T(8,128)(2,1)} %broadcast_select_fusion.17), channel_id=1, source_target_pairs={{0,8},{1,9},{2,10},{3,11},{4,12},{5,13},{6,14},{7,15},{8,0},{9,1},... | collective-permute-start | bytes 393224 | tf_op jit(solution)/shard_map/ppermute | solution.py:13
  58.1 42.2 %collective-permute-start.22 = (bf16[4096,128]{1,0:T(8,128)(2,1)S(1)}, bf16[4096,128]{1,0:T(8,128)(2,1)S(1)}, u32[]{:S(2)}, u32[]{:S(2)}) collective-permute-start(bf16[4096,128]{1,0:T(8,128)(2,1)S(1)} %get-tuple-element.463), channel_id=1, source_target_pairs={{0,2},{1,3},{2,0},{3,1},{4,6},{5,7},{6,4},{7,5},{8,10},{9,11},{10,... | collective-permute-start | bytes 3145736 | tf_op jit(solution)/shard_map/ppermute | solution.py:13
  80.6 20.3 %collective-permute-start.2 = (bf16[4096,128]{1,0:T(8,128)(2,1)S(1)}, bf16[4096,128]{1,0:T(8,128)(2,1)S(1)}, u32[]{:S(2)}, u32[]{:S(2)}) collective-permute-start(bf16[4096,128]{1,0:T(8,128)(2,1)S(1)} %broadcast_select_fusion.9), channel_id=1, source_target_pairs={{0,4},{1,5},{2,6},{3,7},{4,0},{5,1},{6,2},{7,3},{8,12},{9,13},{10,... | collective-permute-start | bytes 3145736 | tf_op jit(solution)/shard_map/ppermute | solution.py:13
  100.3 37.3 %collective-permute-start.13 = (bf16[4096,128]{1,0:T(8,128)(2,1)S(1)}, bf16[4096,128]{1,0:T(8,128)(2,1)S(1)}, u32[]{:S(2)}, u32[]{:S(2)}) collective-permute-start(bf16[4096,128]{1,0:T(8,128)(2,1)S(1)} %broadcast_select_fusion.5), channel_id=1, source_target_pairs={{0,4},{1,5},{2,6},{3,7},{4,0},{5,1},{6,2},{7,3},{8,12},{9,13},{10,... | collective-permute-start | bytes 3145736 | tf_op jit(solution)/shard_map/ppermute | solution.py:13
  100.9 58.9 %collective-permute-start.23 = (bf16[4096,128]{1,0:T(8,128)(2,1)S(1)}, bf16[4096,128]{1,0:T(8,128)(2,1)S(1)}, u32[]{:S(2)}, u32[]{:S(2)}) collective-permute-start(bf16[4096,128]{1,0:T(8,128)(2,1)S(1)} %broadcast_select_fusion.1), channel_id=1, source_target_pairs={{0,4},{1,5},{2,6},{3,7},{4,0},{5,1},{6,2},{7,3},{8,12},{9,13},{10,... | collective-permute-start | bytes 3145736 | tf_op jit(solution)/shard_map/ppermute | solution.py:13
  137.6 79.3 %collective-permute-start.3 = (bf16[4096,128]{1,0:T(8,128)(2,1)S(1)}, bf16[4096,128]{1,0:T(8,128)(2,1)S(1)}, u32[]{:S(2)}, u32[]{:S(2)}) collective-permute-start(bf16[4096,128]{1,0:T(8,128)(2,1)S(1)} %broadcast_select_fusion.10), channel_id=1, source_target_pairs={{0,8},{1,9},{2,10},{3,11},{4,12},{5,13},{6,14},{7,15},{8,0},{9,1},... | collective-permute-start | bytes 3145736 | tf_op jit(solution)/shard_map/ppermute | solution.py:13
  159.8 130.1 %collective-permute-start.14 = (bf16[4096,128]{1,0:T(8,128)(2,1)}, bf16[4096,128]{1,0:T(8,128)(2,1)}, u32[]{:S(2)}, u32[]{:S(2)}) collective-permute-start(bf16[4096,128]{1,0:T(8,128)(2,1)} %broadcast_select_fusion.6), channel_id=1, source_target_pairs={{0,8},{1,9},{2,10},{3,11},{4,12},{5,13},{6,14},{7,15},{8,0},{9,1},... | collective-permute-start | bytes 3145736 | tf_op jit(solution)/shard_map/ppermute | solution.py:13
  216.9 145.7 %collective-permute-start.24 = (bf16[4096,128]{1,0:T(8,128)(2,1)}, bf16[4096,128]{1,0:T(8,128)(2,1)}, u32[]{:S(2)}, u32[]{:S(2)}) collective-permute-start(bf16[4096,128]{1,0:T(8,128)(2,1)} %broadcast_select_fusion.2), channel_id=1, source_target_pairs={{0,8},{1,9},{2,10},{3,11},{4,12},{5,13},{6,14},{7,15},{8,0},{9,1},... | collective-permute-start | bytes 3145736 | tf_op jit(solution)/shard_map/ppermute | solution.py:13
  289.2 145.7 %collective-permute-start.8 = (f32[16,4096]{1,0:T(8,128)}, f32[16,4096]{1,0:T(8,128)}, u32[]{:S(2)}, u32[]{:S(2)}) collective-permute-start(f32[16,4096]{1,0:T(8,128)} %get-tuple-element.248), channel_id=1, source_target_pairs={{0,1},{1,0},{2,3},{3,2},{4,5},{5,4},{6,7},{7,6},{8,9},{9,8},{10,11... | collective-permute-start | bytes 786440 | tf_op jit(solution)/shard_map/ppermute | solution.py:13
  361.9 74.9 %collective-permute-start.18 = (f32[16,4096]{1,0:T(8,128)}, f32[16,4096]{1,0:T(8,128)}, u32[]{:S(2)}, u32[]{:S(2)}) collective-permute-start(f32[16,4096]{1,0:T(8,128)} %get-tuple-element.250), channel_id=1, source_target_pairs={{0,1},{1,0},{2,3},{3,2},{4,5},{5,4},{6,7},{7,6},{8,9},{9,8},{10,11... | collective-permute-start | bytes 786440 | tf_op jit(solution)/shard_map/ppermute | solution.py:13
  437.8 12.8 %collective-permute-start.19 = (f32[16,4096]{1,0:T(8,128)S(1)}, f32[16,4096]{1,0:T(8,128)S(1)}, u32[]{:S(2)}, u32[]{:S(2)}) collective-permute-start(f32[16,4096]{1,0:T(8,128)S(1)} %broadcast_select_fusion.18), channel_id=1, source_target_pairs={{0,2},{1,3},{2,0},{3,1},{4,6},{5,7},{6,4},{7,5},{8,10},{9,11},{10,... | collective-permute-start | bytes 786440 | tf_op jit(solution)/shard_map/ppermute | solution.py:13
  439.1 16.8 %collective-permute-start.29 = (f32[16,4096]{1,0:T(8,128)S(1)}, f32[16,4096]{1,0:T(8,128)S(1)}, u32[]{:S(2)}, u32[]{:S(2)}) collective-permute-start(f32[16,4096]{1,0:T(8,128)S(1)} %broadcast_select_fusion.12), channel_id=1, source_target_pairs={{0,2},{1,3},{2,0},{3,1},{4,6},{5,7},{6,4},{7,5},{8,10},{9,11},{10,... | collective-permute-start | bytes 786440 | tf_op jit(solution)/shard_map/ppermute | solution.py:13
  445.1 10.9 %collective-permute-start.10 = (f32[16,4096]{1,0:T(8,128)S(1)}, f32[16,4096]{1,0:T(8,128)S(1)}, u32[]{:S(2)}, u32[]{:S(2)}) collective-permute-start(f32[16,4096]{1,0:T(8,128)S(1)} %broadcast_select_fusion.26), channel_id=1, source_target_pairs={{0,4},{1,5},{2,6},{3,7},{4,0},{5,1},{6,2},{7,3},{8,12},{9,13},{10,... | collective-permute-start | bytes 786440 | tf_op jit(solution)/shard_map/ppermute | solution.py:13
  455.9 9.2 %collective-permute-start.30 = (f32[16,4096]{1,0:T(8,128)S(1)}, f32[16,4096]{1,0:T(8,128)S(1)}, u32[]{:S(2)}, u32[]{:S(2)}) collective-permute-start(f32[16,4096]{1,0:T(8,128)S(1)} %broadcast_select_fusion.14), channel_id=1, source_target_pairs={{0,4},{1,5},{2,6},{3,7},{4,0},{5,1},{6,2},{7,3},{8,12},{9,13},{10,... | collective-permute-start | bytes 786440 | tf_op jit(solution)/shard_map/ppermute | solution.py:13
  456.1 42.1 %collective-permute-start.11 = (f32[16,4096]{1,0:T(8,128)S(1)}, f32[16,4096]{1,0:T(8,128)S(1)}, u32[]{:S(2)}, u32[]{:S(2)}) collective-permute-start(f32[16,4096]{1,0:T(8,128)S(1)} %broadcast_select_fusion.28), channel_id=1, source_target_pairs={{0,8},{1,9},{2,10},{3,11},{4,12},{5,13},{6,14},{7,15},{8,0},{9,1},... | collective-permute-start | bytes 786440 | tf_op jit(solution)/shard_map/ppermute | solution.py:13
  458.3 39.8 %collective-permute-start.21 = (f32[16,4096]{1,0:T(8,128)S(1)}, f32[16,4096]{1,0:T(8,128)S(1)}, u32[]{:S(2)}, u32[]{:S(2)}) collective-permute-start(f32[16,4096]{1,0:T(8,128)S(1)} %broadcast_select_fusion.22), channel_id=1, source_target_pairs={{0,8},{1,9},{2,10},{3,11},{4,12},{5,13},{6,14},{7,15},{8,0},{9,1},... | collective-permute-start | bytes 786440 | tf_op jit(solution)/shard_map/ppermute | solution.py:13
  465.1 33.0 %collective-permute-start.31 = (f32[16,4096]{1,0:T(8,128)S(1)}, f32[16,4096]{1,0:T(8,128)S(1)}, u32[]{:S(2)}, u32[]{:S(2)}) collective-permute-start(f32[16,4096]{1,0:T(8,128)S(1)} %broadcast_select_fusion.16), channel_id=1, source_target_pairs={{0,8},{1,9},{2,10},{3,11},{4,12},{5,13},{6,14},{7,15},{8,0},{9,1},... | collective-permute-start | bytes 786440 | tf_op jit(solution)/shard_map/ppermute | solution.py:13
  (42 other events, 604.0 us)
where the time goes:
time: 500 us; the launch traced here: 499 us
  matrix products  216 us (43%)
  waiting for transfers between devices  199 us (40%)
  starting transfers between devices  25.9 us (5%)
  other arithmetic  24.4 us (5%)
  local copies, waits for them, and re-layouts  23.2 us (5%)
  between operations  10.2 us (2%)
    ppermute x32, waiting for transfers between devices, partner(): return lax.ppermute(value, axis, pairs)  199 us
    dot_general x12, matrix products, kernel_block(): lax.dot_general(row_x, col_x, (((1,), (1,)), ((), ())), preferred_element...  89.4 us
    dot_general x12, matrix products, row_step(): jnp.dot(block_v, kern, preferred_element_type=jnp.float32)  65.3 us
    dot_general x16, matrix products, row_step(): lax.dot_general(col_v, kern, (((1,), (1,)), ((), ())), preferred_element_...  61.4 us
    ppermute x32, starting transfers between devices, partner(): return lax.ppermute(value, axis, pairs)  25.9 us
  transfers between devices with their start and end apart: 32, of which 12 were waited for; matrix products, arithmetic and copies ran while one was open for 51% of the time, Pallas kernels for 0%

commit v1 on v0

v1 whole, which is shorter than its diff:
```python
import functools

import jax
import jax.numpy as jnp
from jax import lax
from jax.experimental import pallas as pl
from jax.experimental.pallas import tpu as pltpu
from jax.sharding import PartitionSpec as P

GAMMA = 2.0
NOISE = 0.25
F32, BF = jnp.float32, jnp.bfloat16


def extend(x_ref, out_ref, scale, own):
    rows, width = x_ref.shape
    chunk = 256

    def step(c, carry):
        r = pl.ds(pl.multiple_of(c * chunk, chunk), chunk)
        xf = x_ref[r, :].astype(F32)
        n = -GAMMA * jnp.sum(xf * xf, axis=1, keepdims=True)
        nh = n.astype(BF).astype(F32)
        rest = n - nh
        nm = rest.astype(BF).astype(F32)
        nl = rest - nm
        lane = lax.broadcasted_iota(jnp.int32, (chunk, 128), 1)
        o = 0 if own else 3
        p = 3 - o
        ones = jnp.where((lane >= p) & (lane < p + 3), 1.0, 0.0)
        extra = jnp.where(
            lane == o,
            nh,
            jnp.where(lane == o + 1, nm, jnp.where(lane == o + 2, nl, ones)),
        )
        out_ref[r, 0:width] = (xf * scale).astype(BF)
        out_ref[r, width : width + 128] = extra.astype(BF)
        return carry

    lax.fori_loop(0, rows // chunk, step, 0)


def tile_kernel(block_i, block_j, idx_ref, far_ref, own_ref, v_ref, start_ref, o_ref, oext, fext):
    rows = own_ref.shape[0]

    @pl.when(pl.program_id(0) == 0)
    def _():
        extend(own_ref, oext, 2 * GAMMA, True)
        o_ref[...] = start_ref[...]

    extend(far_ref, fext, 1.0, False)

    def istep(i, carry):
        ri = pl.ds(pl.multiple_of(i * block_i, block_i), block_i)
        w = oext[ri, :]
        a = o_ref[:, ri]
        for j in range(rows // block_j):
            rj = pl.ds(j * block_j, block_j)
            z = lax.dot_general(
                fext[rj, :], w, (((1,), (1,)), ((), ())), preferred_element_type=F32
            )
            k = jnp.exp(z).astype(BF)
            a = a + jnp.dot(v_ref[:, rj], k, preferred_element_type=F32)
        o_ref[:, ri] = a
        return carry

    lax.fori_loop(0, rows // block_i, istep, 0)


def tiles(idx, far, own, v, start):
    rows, width = own.shape
    probes = start.shape[0]
    count = idx.shape[0]
    n = count * rows * rows
    return pl.pallas_call(
        functools.partial(tile_kernel, 256, 1024),
        out_shape=jax.ShapeDtypeStruct((probes, rows), F32),
        grid_spec=pltpu.PrefetchScalarGridSpec(
            num_scalar_prefetch=1,
            grid=(count,),
            in_specs=[
                pl.BlockSpec((rows, width), lambda t, m: (m[t], 0)),
                pl.BlockSpec((rows, width), lambda t, m: (0, 0)),
                pl.BlockSpec((probes, rows), lambda t, m: (m[t], 0)),
                pl.BlockSpec((probes, rows), lambda t, m: (0, 0)),
            ],
            out_specs=pl.BlockSpec((probes, rows), lambda t, m: (0, 0)),
            scratch_shapes=[
                pltpu.VMEM((rows, width + 128), BF),
                pltpu.VMEM((rows, width + 128), BF),
            ],
        ),
        compiler_params=pltpu.CompilerParams(vmem_limit_bytes=40 << 20),
        cost_estimate=pl.CostEstimate(
            flops=2 * n * (2 * width + 256), bytes_accessed=count * rows * width * 2, transcendentals=n
        ),
    )(idx, far, own, v, start)


def on_device(points, probes, round_masks):
    me = lax.axis_index("dp")
    all_x = lax.all_gather(points, "dp", axis=0, tiled=True)
    all_v = lax.all_gather(probes, "dp", axis=0, tiled=True)
    zero = jnp.zeros((1,), jnp.int32)
    total = tiles(zero, points, points, probes, NOISE * probes.astype(F32))
    return tiles(jnp.bitwise_xor(me, round_masks), all_x, points, all_v, total)


def solution(mesh):
    in_specs = (P(("groups", "dp"), None), P(None, ("groups", "dp")), P("groups"))
    out_specs = P(None, ("groups", "dp"))
    return jax.shard_map(
        on_device, mesh=mesh, in_specs=in_specs, out_specs=out_specs, check_vma=False
    )
```

time: 500 us -> 264 us (0.53)
  matrix products: 216 us -> 0 us
  Pallas kernels: 0 us -> 99.5 us
  waiting for transfers between devices: 199 us -> 146 us
  starting transfers between devices: 25.9 us -> 0.04 us
  other arithmetic: 24.4 us -> 1.58 us
  local copies, waits for them, and re-layouts: 23.2 us -> 3.72 us
    dot_general x40 -> x0, matrix products: 216 us -> none  [the longest x12 89.4 us: kernel_block(): lax.dot_general(row_x, col_x, (((1,), (1,)), ((), ())), preferred_element...]
    ppermute x32 -> x0, waiting for transfers between devices: 199 us -> none  [partner(): return lax.ppermute(value, axis, pairs)]
    all_gather x0 -> x2, waiting for transfers between devices: none -> 145 us  [the longest x1 128 us: on_device(): all_x = lax.all_gather(points, 'dp', axis=0, tiled=True)]
    pallas_call x0 -> x2, Pallas kernels: none -> 99.5 us  [tiles(): pl.pallas_call(functools.partial(tile_kernel, 256, 1024), out_shape=jax.S...]
    ppermute x32 -> x0, starting transfers between devices: 25.9 us -> none  [partner(): return lax.ppermute(value, axis, pairs)]
    select_n x26 -> x0, other arithmetic: 12 us -> none  [the longest x10 5.49 us: fetch_partner(): jnp.where(bitset, moved[1], pair[1])]
    while x48 -> x0, local copies, waits for them, and re-layouts: 6.66 us -> none
    convert_element_type x3 -> x0, other arithmetic: 6.06 us -> none  [point_norms(): return jnp.sum(jnp.square(rows.astype(jnp.float32)), axis=1)]
  transfers between devices with their start and end apart: 32 -> 2, of which waited for: 12 -> 2; matrix products, arithmetic and copies ran while one was open for 51% -> 1% of each run, Pallas kernels for 0% -> 10%
where the time goes in v1:
time: 264 us
  waiting for transfers between devices  146 us (55%)
  Pallas kernels  99.5 us (38%)
  between operations  13.4 us (5%)
  local copies, waits for them, and re-layouts  3.72 us (1%)
    all_gather x1, waiting for transfers between devices, on_device(): all_x = lax.all_gather(points, 'dp', axis=0, tiled=True)  128 us
    pallas_call x2, Pallas kernels, tiles(): pl.pallas_call(functools.partial(tile_kernel, 256, 1024), out_shape=jax.S...  99.5 us
    all_gather x1, waiting for transfers between devices, on_device(): all_v = lax.all_gather(probes, 'dp', axis=0, tiled=True)  16.7 us
  transfers between devices with their start and end apart: 2, of which 2 were waited for; matrix products, arithmetic and copies ran while one was open for 1% of the time, Pallas kernels for 10%

profile of v1, /device:TPU:0, one launch (start us, length us, event | category | flops | bytes accessed | tf_op | source)
XLA Modules:
  0.0 264.2 jit_solution(17969858171452671662)
XLA Ops:
  6.5 0.0 all-gather.5.cloned.1.call-start
  6.5 0.7 all-gather.5.cloned.1.call-update
  7.3 0.0 all-gather.3.cloned.1.call-start
  7.3 0.7 all-gather.3.cloned.1.call-update
  8.0 0.7 broadcast_xor_fusion.idx_ref
  8.7 0.9 convert_multiply_fusion.start_ref
  9.6 0.0 copy-start
  9.6 1.2 copy-done
  10.8 0.0 copy-start.2
  10.8 0.9 copy-done.2
  11.7 0.0 copy-start.1
  11.7 25.3 %shard_map.37.start_ref = f32[16,4096]{1,0:T(8,128)S(1)} custom-call(s32[1]{0:T(128)} %constant.1.clone.1.idx_ref, bf16[4096,128]{1,0:T(8,128)(2,1)S(1)} %copy-done, bf16[4096,128]{1,0:T(8,128)(2,1)S(1)} %copy-done, bf16[16,4096]{1,0:T(8,128)(2,1)S(1)} %copy-done.2, f32[16,4096]{1,0:T(8,128)S(1)} %convert_multiply_fusion.start_ref), custom_call_target="tpu_custom_call" | custom-call | flops 17179869184 | bytes 1048576 | tf_op jit(solution)/shard_map/pallas_call | solution.py:75
  37.0 16.7 %all-gather.5.cloned.1.call-done.v_ref = bf16[256,4096]{1,0:T(8,128)(2,1)} async-done(((bf16[16,4096]{1,0:T(8,128)(2,1)}), bf16[256,4096]{1,0:T(8,128)(2,1)}) %all-gather.5.cloned.1.call-update) | async-done | bytes 2097168 | tf_op jit(solution)/shard_map/all_gather | solution.py:103
  53.7 127.8 %all-gather.3.cloned.1.call-done.far_ref = bf16[65536,128]{1,0:T(8,128)(2,1)} async-done(((bf16[4096,128]{1,0:T(8,128)(2,1)}), bf16[65536,128]{1,0:T(8,128)(2,1)}) %all-gather.3.cloned.1.call-update) | async-done | bytes 16777232 | tf_op jit(solution)/shard_map/all_gather | solution.py:102
  181.5 0.0 copy-done.1
  181.5 0.0 copy-start.3
  181.5 1.6 copy-done.3
  183.1 74.2 %shard_map.38 = f32[16,4096]{1,0:T(8,128)} custom-call(s32[3]{0:T(128)S(1)} %broadcast_xor_fusion.idx_ref, bf16[65536,128]{1,0:T(8,128)(2,1)} %all-gather.3.cloned.1.call-done.far_ref, bf16[4096,128]{1,0:T(8,128)(2,1)S(1)} %copy-done.1, bf16[256,4096]{1,0:T(8,128)(2,1)S(1)} %copy-done.3, f32[16,4096]{1,0:T(8,128)S(1)} %shard_map.37.start_ref), custom_call_target="tpu_custom_call" | custom-call | flops 51539607552 | bytes 3145728 | tf_op jit(solution)/shard_map/pallas_call | solution.py:75
Async XLA Ops:
  6.5 47.2 %all-gather.5.cloned.1.call-start = ((), (), s32[]{:S(2)}) async-start(), calls=%async_computation.1 | async-start | bytes 2228224 | tf_op jit(solution)/shard_map/all_gather | solution.py:103
  7.3 174.3 %all-gather.3.cloned.1.call-start = ((), (), s32[]{:S(2)}) async-start(), calls=%async_computation | async-start | bytes 17825792 | tf_op jit(solution)/shard_map/all_gather | solution.py:102
  9.6 1.2 copy-start
  10.8 0.9 copy-start.2
  11.7 169.8 %copy-start.1 = (bf16[4096,128]{1,0:T(8,128)(2,1)S(1)}, bf16[4096,128]{1,0:T(8,128)(2,1)}, u32[]{:S(2)}) copy-start(bf16[4096,128]{1,0:T(8,128)(2,1)} %own_ref.3) | copy-start | bytes 3145732
  181.5 1.6 copy-start.3
Sparse Core Ops, SparseCore 0:
  9.5 44.1 all-gather.4
  55.9 125.6 all-gather.2

commit v2 on v1

v2 whole, which is shorter than its diff:
```python
import functools

import jax
import jax.numpy as jnp
from jax import lax
from jax.experimental import pallas as pl
from jax.experimental.pallas import tpu as pltpu
from jax.sharding import PartitionSpec as P

GAMMA = 2.0
NOISE = 0.25
F32, BF = jnp.float32, jnp.bfloat16
BLOCK_I = 512


def extended(x, scale, own):
    xf = x.astype(F32)
    n = -GAMMA * jnp.sum(xf * xf, axis=1, keepdims=True)
    nh = n.astype(BF).astype(F32)
    rest = n - nh
    nm = rest.astype(BF).astype(F32)
    nl = rest - nm
    lane = lax.broadcasted_iota(jnp.int32, (x.shape[0], 128), 1)
    o = 0 if own else 3
    p = 3 - o
    ones = jnp.where((lane >= p) & (lane < p + 3), 1.0, 0.0)
    extra = jnp.where(
        lane == o,
        nh,
        jnp.where(lane == o + 1, nm, jnp.where(lane == o + 2, nl, ones)),
    )
    return (xf * scale).astype(BF), extra.astype(BF)


def kernel(n, idx_ref, x_ref, v_ref, o_ref, xe, xl, ve, vl, oext, fext, vs,
           ring_send, ring_recv, sib_send, sib_recv):
    rows, width = x_ref.shape
    half = rows // 2
    chips = n // 2
    depth = chips // 2
    me = lax.axis_index("dp")
    chip, core = me // 2, me % 2

    z, y = chip // 2, chip % 2
    pos = (1 - y) * z + y * (chips - 1 - z)

    def device_at(q, c):
        q = lax.rem(q + 2 * chips, chips)
        second = q // depth
        qz = (1 - second) * q + second * (chips - 1 - q)
        return (qz * 2 + second) * 2 + c

    right, left = device_at(pos + 1, core), device_at(pos - 1, core)
    sibling = device_at(pos, 1 - core)

    barrier = pltpu.get_barrier_semaphore()
    for other in (right, left, sibling):
        pl.semaphore_signal(
            barrier, inc=1, device_id={"dp": other}, device_id_type=pl.DeviceIdType.MESH
        )

    def remote(src, dst, send, recv, to):
        return pltpu.make_async_remote_copy(
            src_ref=src, dst_ref=dst, send_sem=send, recv_sem=recv,
            device_id={"dp": to}, device_id_type=pl.DeviceIdType.MESH,
        )

    def slots(direction, distance):
        early = distance <= depth if direction == 0 else distance < depth
        return (xe, ve) if early else (xl, vl)

    def own_half(h):
        return (x_ref.at[pl.ds(h * half, half), :], v_ref.at[:, pl.ds(h * half, half)])

    pending = []

    def ring(direction, step):
        sign = 1 - 2 * direction
        blk = device_at(pos - sign * step, core)
        if step == 0:
            source = own_half(direction)
        else:
            bx, bv = slots(direction, step)
            source = (bx.at[blk], bv.at[blk])
        dx, dv = slots(direction, step + 1)
        to = right if direction == 0 else left
        out = []
        for k, (s, d) in enumerate(zip(source, (dx, dv))):
            c = remote(s, d.at[blk], ring_send.at[direction, step, k],
                       ring_recv.at[direction, step, k], to)
            c.start()
            out.append(c)
            pending.append(c)
        return out

    def pass_on(direction, step):
        sign = 1 - 2 * direction
        blk = device_at(pos - sign * step, core)
        if step == 0:
            source = own_half(direction)
            dx, dv = (xe, ve) if direction == 0 else (xl, vl)
        else:
            dx, dv = slots(direction, step)
            source = (dx.at[blk], dv.at[blk])
        out = []
        for k, (s, d) in enumerate(zip(source, (dx, dv))):
            c = remote(s, d.at[blk], sib_send.at[direction, step, k],
                       sib_recv.at[direction, step, k], sibling)
            c.start()
            out.append(c)
            pending.append(c)
        return out

    pl.semaphore_wait(barrier, 3)
    moving = [ring(0, 0), ring(1, 0)]
    from_sibling = [pass_on(0, 0), pass_on(1, 0)]

    def advance(step):
        for direction in range(2):
            for c in moving[direction]:
                c.wait_recv()
            if step < chips - 1:
                moving[direction] = ring(direction, step)
            from_sibling.append(pass_on(direction, step))

    def sibling_done():
        for copies in from_sibling:
            for c in copies:
                c.wait_recv()
        from_sibling.clear()

    chunk = 256

    def far(load):
        def step(c, carry):
            r = pl.ds(pl.multiple_of(c * chunk, chunk), chunk)
            a, b = extended(load(r), 1.0, False)
            fext[r, 0:width] = a
            fext[r, width:] = b
            return carry

        lax.fori_loop(0, half // chunk, step, 0)

    def product(first=0, last=rows // BLOCK_I):
        def istep(i, carry):
            ri = pl.ds(pl.multiple_of(i * BLOCK_I, BLOCK_I), BLOCK_I)
            s = lax.dot_general(
                fext[...], oext[ri, :], (((1,), (1,)), ((), ())), preferred_element_type=F32
            )
            k = jnp.exp(s).astype(BF)
            o_ref[:, ri] += jnp.dot(vs[...], k, preferred_element_type=F32)
            return carry

        lax.fori_loop(first, last, istep, 0)

    def tile(bx, bv, i):
        far(lambda r: bx[i, r, :])
        vs[...] = bv[i]
        product()

    def own_step(c, carry):
        r = pl.ds(pl.multiple_of(c * chunk, chunk), chunk)
        a, b = extended(x_ref[r, :], 2 * GAMMA, True)
        oext[r, 0:width] = a
        oext[r, width:] = b
        return carry

    lax.fori_loop(0, rows // chunk, own_step, 0)
    o_ref[...] = NOISE * v_ref[...].astype(F32)

    def own_tile(h):
        far(lambda r: x_ref[pl.ds(pl.multiple_of(r.start + h * half, chunk), chunk), :])
        vs[...] = v_ref[:, h * half:(h + 1) * half]
        product()

    own_tile(0)
    advance(1)
    own_tile(1)
    for step in range(2, depth + 1):
        advance(step)
    sibling_done()
    across = device_at(pos + depth, 1 - core)
    first, second = idx_ref[0], idx_ref[1]
    work = [
        lambda: tile(xe, ve, across),
        lambda: tile(xl, vl, across),
        lambda: tile(xe, ve, first),
        lambda: tile(xe, ve, second),
    ]
    for step in range(depth + 1, chips):
        if work:
            work.pop(0)()
        advance(step)
    for todo in work:
        todo()
    sibling_done()
    tile(xl, vl, first)
    tile(xl, vl, second)
    for c in pending:
        c.wait_send()


def on_device(n, points, probes, round_masks):
    rows, width = points.shape
    probe_count = probes.shape[0]
    me = lax.axis_index("dp")
    low = jnp.min(round_masks)
    mid = jnp.sum(round_masks) - low - jnp.max(round_masks)
    idx = jnp.bitwise_xor(me, jnp.stack([low, mid]))
    chips = n // 2
    vmem = pl.BlockSpec(memory_space=pltpu.VMEM)
    dots = 4 * rows * rows
    return pl.pallas_call(
        functools.partial(kernel, n),
        out_shape=jax.ShapeDtypeStruct((probe_count, rows), F32),
        in_specs=[pl.BlockSpec(memory_space=pltpu.SMEM), vmem, vmem],
        out_specs=vmem,
        scratch_shapes=[
            pltpu.VMEM((n, rows // 2, width), BF),
            pltpu.VMEM((n, rows // 2, width), BF),
            pltpu.VMEM((n, probe_count, rows // 2), BF),
            pltpu.VMEM((n, probe_count, rows // 2), BF),
            pltpu.VMEM((rows, width + 128), BF),
            pltpu.VMEM((rows // 2, width + 128), BF),
            pltpu.VMEM((probe_count, rows // 2), BF),
            pltpu.SemaphoreType.DMA((2, chips - 1, 2)),
            pltpu.SemaphoreType.DMA((2, chips - 1, 2)),
            pltpu.SemaphoreType.DMA((2, chips, 2)),
            pltpu.SemaphoreType.DMA((2, chips, 2)),
        ],
        compiler_params=pltpu.CompilerParams(
            collective_id=0, has_side_effects=True, vmem_limit_bytes=60 << 20
        ),
        cost_estimate=pl.CostEstimate(
            flops=2 * dots * (width + 16), bytes_accessed=2 * rows * width, transcendentals=dots
        ),
    )(idx, points, probes)


def solution(mesh):
    in_specs = (P(("groups", "dp"), None), P(None, ("groups", "dp")), P("groups"))
    out_specs = P(None, ("groups", "dp"))
    return jax.shard_map(
        functools.partial(on_device, mesh.shape["dp"]),
        mesh=mesh, in_specs=in_specs, out_specs=out_specs, check_vma=False,
    )
```

time: 264 us -> 136 us (0.52)
  waiting for transfers between devices: 146 us -> 0 us
  Pallas kernels: 99.5 us -> 129 us
  between operations: 13.4 us -> 1.91 us
    all_gather x2 -> x0, waiting for transfers between devices: 145 us -> none  [the longest x1 128 us: on_device(): all_x = lax.all_gather(points, 'dp', axis=0, tiled=True)]
    pallas_call x2 -> x1, Pallas kernels: 99.5 us -> 129 us  [on_device(): pl.pallas_call(functools.partial(kernel, n), out_shape=jax.ShapeDtypeStru...]
  transfers between devices with their start and end apart: 2 -> 0, of which waited for: 2 -> 0; matrix products, arithmetic and copies ran while one was open for 1% -> 0% of each run, Pallas kernels for 10% -> 0%
where the time goes in v2:
time: 136 us; the launch traced here: 135 us
  Pallas kernels  129 us (95%)
  local copies, waits for them, and re-layouts  2.33 us (2%)
  other arithmetic  2.05 us (2%)
  between operations  1.91 us (1%)
    pallas_call x1, Pallas kernels, on_device(): pl.pallas_call(functools.partial(kernel, n), out_shape=jax.ShapeDtypeStru...  129 us

profile of v2, /device:TPU:0, one launch (start us, length us, event | category | flops | bytes accessed | tf_op | source)
XLA Modules:
  0.0 135.5 jit_solution(5556566793168607331)
XLA Ops:
  0.0 0.0 copy-start
  0.0 0.7 copy-done
  0.7 0.7 fusion
  3.3 1.3 add_xor_fusion.idx_ref
  4.6 129.2 %shard_map.37 = f32[16,4096]{1,0:T(8,128)} custom-call(s32[2]{0:T(128)} %add_xor_fusion.idx_ref, bf16[4096,128]{1,0:T(8,128)(2,1)} %x_ref.1, bf16[16,4096]{1,0:T(8,128)(2,1)} %v_ref.1), custom_call_target="tpu_custom_call" | custom-call | flops 19327352832 | bytes 1048576 | tf_op jit(solution)/shard_map/pallas_call | solution.py:213
  133.8 1.7 %copy.5 = f32[16,4096]{1,0:T(8,128)} copy(f32[16,4096]{1,0:T(8,128)} %shard_map.37) | data formatting | bytes 524288
Async XLA Ops:
  0.0 0.7 copy-start

commit v3 on v2

--- a/solution.py
+++ b/solution.py
@@ -10,7 +10,8 @@
 GAMMA = 2.0
 NOISE = 0.25
 F32, BF = jnp.float32, jnp.bfloat16
-BLOCK_I = 512
+BLOCK_I = 1024
+PIECES = 2
 
 
 def extended(x, scale, own):
@@ -36,6 +37,7 @@
            ring_send, ring_recv, sib_send, sib_recv):
     rows, width = x_ref.shape
     half = rows // 2
+    part = half // PIECES
     chips = n // 2
     depth = chips // 2
     me = lax.axis_index("dp")
@@ -69,59 +71,56 @@
         early = distance <= depth if direction == 0 else distance < depth
         return (xe, ve) if early else (xl, vl)
 
-    def own_half(h):
-        return (x_ref.at[pl.ds(h * half, half), :], v_ref.at[:, pl.ds(h * half, half)])
+    def piece(h, k):
+        at = h * half + k * part
+        return x_ref.at[pl.ds(at, part), :], v_ref.at[:, pl.ds(at, part)]
+
+    def held(refs, blk, k):
+        bx, bv = refs
+        return bx.at[blk, pl.ds(k * part, part), :], bv.at[blk, :, pl.ds(k * part, part)]
 
     pending = []
 
-    def ring(direction, step):
-        sign = 1 - 2 * direction
-        blk = device_at(pos - sign * step, core)
-        if step == 0:
-            source = own_half(direction)
-        else:
-            bx, bv = slots(direction, step)
-            source = (bx.at[blk], bv.at[blk])
-        dx, dv = slots(direction, step + 1)
-        to = right if direction == 0 else left
+    def send(source, target, sends, recvs, at, to):
         out = []
-        for k, (s, d) in enumerate(zip(source, (dx, dv))):
-            c = remote(s, d.at[blk], ring_send.at[direction, step, k],
-                       ring_recv.at[direction, step, k], to)
+        for j, (s, d) in enumerate(zip(source, target)):
+            c = remote(s, d, sends.at[at + (j,)], recvs.at[at + (j,)], to)
             c.start()
             out.append(c)
             pending.append(c)
         return out
 
-    def pass_on(direction, step):
-        sign = 1 - 2 * direction
-        blk = device_at(pos - sign * step, core)
+    def block_back(direction, step):
+        return device_at(pos - (1 - 2 * direction) * step, core)
+
+    def ring(direction, step, k):
+        blk = block_back(direction, step)
+        source = piece(direction, k) if step == 0 else held(slots(direction, step), blk, k)
+        target = held(slots(direction, step + 1), blk, k)
+        return send(source, target, ring_send, ring_recv, (direction, step, k),
+                    left if direction else right)
+
+    def pass_on(direction, step, k):
+        blk = block_back(direction, step)
         if step == 0:
-            source = own_half(direction)
-            dx, dv = (xe, ve) if direction == 0 else (xl, vl)
+            source, refs = piece(direction, k), (xl, vl) if direction else (xe, ve)
         else:
-            dx, dv = slots(direction, step)
-            source = (dx.at[blk], dv.at[blk])
-        out = []
-        for k, (s, d) in enumerate(zip(source, (dx, dv))):
-            c = remote(s, d.at[blk], sib_send.at[direction, step, k],
-                       sib_recv.at[direction, step, k], sibling)
-            c.start()
-            out.append(c)
-            pending.append(c)
-        return out
+            refs = slots(direction, step)
+            source = held(refs, blk, k)
+        return send(source, held(refs, blk, k), sib_send, sib_recv, (direction, step, k), sibling)
 
     pl.semaphore_wait(barrier, 3)
-    moving = [ring(0, 0), ring(1, 0)]
-    from_sibling = [pass_on(0, 0), pass_on(1, 0)]
+    pieces = [(k, direction) for k in range(PIECES) for direction in range(2)]
+    moving = {(k, direction): ring(direction, 0, k) for k, direction in pieces}
+    from_sibling = [pass_on(direction, 0, k) for k, direction in pieces]
 
     def advance(step):
-        for direction in range(2):
-            for c in moving[direction]:
+        for k, direction in pieces:
+            for c in moving[k, direction]:
                 c.wait_recv()
             if step < chips - 1:
-                moving[direction] = ring(direction, step)
-            from_sibling.append(pass_on(direction, step))
+                moving[k, direction] = ring(direction, step, k)
+            from_sibling.append(pass_on(direction, step, k))
 
     def sibling_done():
         for copies in from_sibling:
@@ -223,10 +222,10 @@
             pltpu.VMEM((rows, width + 128), BF),
             pltpu.VMEM((rows // 2, width + 128), BF),
             pltpu.VMEM((probe_count, rows // 2), BF),
-            pltpu.SemaphoreType.DMA((2, chips - 1, 2)),
-            pltpu.SemaphoreType.DMA((2, chips - 1, 2)),
-            pltpu.SemaphoreType.DMA((2, chips, 2)),
-            pltpu.SemaphoreType.DMA((2, chips, 2)),
+            pltpu.SemaphoreType.DMA((2, chips - 1, PIECES, 2)),
+            pltpu.SemaphoreType.DMA((2, chips - 1, PIECES, 2)),
+            pltpu.SemaphoreType.DMA((2, chips, PIECES, 2)),
+            pltpu.SemaphoreType.DMA((2, chips, PIECES, 2)),
         ],
         compiler_params=pltpu.CompilerParams(
             collective_id=0, has_side_effects=True, vmem_limit_bytes=60 << 20

time: 136 us -> 129 us (0.949)
  Pallas kernels: 129 us -> 122 us
    pallas_call x1, Pallas kernels: 129 us -> 122 us  [on_device(): pl.pallas_call(functools.partial(kernel, n), out_shape=jax.ShapeDtypeStru...]
where the time goes in v3:
time: 129 us; the launch traced here: 128 us
  Pallas kernels  122 us (95%)
  local copies, waits for them, and re-layouts  2.33 us (2%)
  other arithmetic  2.05 us (2%)
  between operations  1.91 us (1%)
    pallas_call x1, Pallas kernels, on_device(): pl.pallas_call(functools.partial(kernel, n), out_shape=jax.ShapeDtypeStru...  122 us

profile of v3, /device:TPU:0, one launch (start us, length us, event | category | flops | bytes accessed | tf_op | source)
XLA Modules:
  0.0 128.2 jit_solution(8696782221437463235)
XLA Ops:
  0.0 0.0 copy-start
  0.0 0.7 copy-done
  0.7 0.7 fusion
  3.3 1.3 %add_xor_fusion.idx_ref = s32[2]{0:T(128)} fusion(s32[1]{0:T(128)} %bitcast.1, s32[1]{0:T(128)} %bitcast, s32[]{:T(128)S(6)} %axis_index.12), kind=kLoop, calls=%fused_computation | loop fusion | flops 4 | bytes 20 | tf_op jit(solution)/shard_map/xor | solution.py:208
  4.6 121.9 %shard_map.37 = f32[16,4096]{1,0:T(8,128)} custom-call(s32[2]{0:T(128)} %add_xor_fusion.idx_ref, bf16[4096,128]{1,0:T(8,128)(2,1)} %x_ref.1, bf16[16,4096]{1,0:T(8,128)(2,1)} %v_ref.1), custom_call_target="tpu_custom_call" | custom-call | flops 19327352832 | bytes 1048576 | tf_op jit(solution)/shard_map/pallas_call | solution.py:212
  126.5 1.7 %copy.5 = f32[16,4096]{1,0:T(8,128)} copy(f32[16,4096]{1,0:T(8,128)} %shard_map.37) | data formatting | bytes 524288
Async XLA Ops:
  0.0 0.7 copy-start
